TPU v7x, 128 devices: a whole 4x4x4 slice. The times are simulated.
128 devices in a mesh: gx: 4 (over y), gy: 4 (over x_hi, core), gz: 8 (over x_lo, z).
Axes of the slice: x: 4 (x_hi: 2, x_lo: 2; x = x_hi * 2 + x_lo), y: 4, z: 4, core: 2. Of those that a mesh axis runs over, the one named last changes fastest.
Arguments:
- tokens: bfloat16 [64, 64, 128, 256], P('gx', 'gy', 'gz'), may hold values from -17 to 17, as said below
- grad_out: bfloat16 [64, 64, 128, 256], P('gx', 'gy', 'gz'), may hold values from -6 to 6
- w_qkv: bfloat16 [256, 768], replicated, may hold values from -0.375 to 0.375
- w_out: bfloat16 [256, 256], replicated, may hold values from -0.375 to 0.375
Outputs:
- grad_tokens: bfloat16 [64, 64, 128, 256], P('gx', 'gy', 'gz')
- grad_qkv_weight: float32 [256, 768], replicated
- grad_out_weight: float32 [256, 256], replicated
Inputs may be any that keep to these rules, and one draw needn't show every extreme that they name: `tokens`: entries of order one, each token row multiplied by its own positive scale.
All inputs are finite; a program needn't handle non-finite values.
Results may differ from a plain program's by a relative error of at most 0.015.
Values may be sent and summed in bfloat16 or wider, within the bound.
A program may use at most 128 MiB of HBM per device.

v0:
```python
import math

import jax
import jax.numpy as jnp
from jax import lax
from jax.sharding import PartitionSpec as P

HEADS = 8
HEAD_DIM = 32
GRID = 4


def to_windows(stacked):
    layers, edge_x, edge_y, edge_z, width = stacked.shape
    size_x, size_y, size_z = (lax.axis_size("gx"), lax.axis_size("gy"), lax.axis_size("gz"))
    inner = (layers, edge_x // size_x, edge_y // size_y, edge_z // size_z, width)
    arranged = stacked.reshape(
        layers, edge_x // size_x, size_x, edge_y // size_y, size_y, edge_z // size_z, size_z, width
    )
    arranged = arranged.transpose(2, 4, 6, 0, 1, 3, 5, 7)
    arranged = lax.all_to_all(
        arranged.reshape((size_x * size_y * size_z,) + inner),
        ("gx", "gy", "gz"),
        split_axis=0,
        concat_axis=0,
        tiled=True,
    )
    arranged = arranged.reshape((size_x, size_y, size_z) + inner)
    arranged = arranged.transpose(3, 0, 4, 1, 5, 2, 6, 7)
    arranged = arranged.reshape(
        layers, GRID, edge_x // GRID, GRID, edge_y // GRID, GRID, edge_z // GRID, width
    )
    arranged = arranged.transpose(0, 2, 4, 6, 1, 3, 5, 7)
    return arranged.reshape(layers, -1, GRID**3, width)


def from_windows(stacked, edges):
    layers, width = (stacked.shape[0], stacked.shape[-1])
    edge_x, edge_y, edge_z = edges
    size_x, size_y, size_z = (lax.axis_size("gx"), lax.axis_size("gy"), lax.axis_size("gz"))
    inner = (layers, edge_x // size_x, edge_y // size_y, edge_z // size_z, width)
    arranged = stacked.reshape(
        layers, edge_x // GRID, edge_y // GRID, edge_z // GRID, GRID, GRID, GRID, width
    )
    arranged = arranged.transpose(0, 4, 1, 5, 2, 6, 3, 7)
    arranged = arranged.reshape(
        layers, size_x, edge_x // size_x, size_y, edge_y // size_y, size_z, edge_z // size_z, width
    )
    arranged = arranged.transpose(1, 3, 5, 0, 2, 4, 6, 7)
    arranged = lax.all_to_all(
        arranged.reshape((size_x * size_y * size_z,) + inner),
        ("gx", "gy", "gz"),
        split_axis=0,
        concat_axis=0,
        tiled=True,
    )
    arranged = arranged.reshape((size_x, size_y, size_z) + inner)
    arranged = arranged.transpose(3, 4, 0, 5, 1, 6, 2, 7)
    return arranged.reshape(layers, edge_x, edge_y, edge_z, width)


def attend(queries, key_rows, values, grad_mixed):
    count, members, width = queries.shape
    scaling = HEAD_DIM ** (-0.5)
    query_heads = queries.reshape(count, members, HEADS, HEAD_DIM)
    key_heads = key_rows.reshape(count, members, HEADS, HEAD_DIM)
    value_heads = values.reshape(count, members, HEADS, HEAD_DIM)
    grad_heads = grad_mixed.reshape(count, members, HEADS, HEAD_DIM)
    scores = (
        jnp.einsum("wqhc,wkhc->whqk", query_heads, key_heads, preferred_element_type=jnp.float32)
        * scaling
    )
    attention = jax.nn.softmax(scores, axis=-1)
    attention_b = attention.astype(jnp.bfloat16)
    mixed = jnp.einsum(
        "whqk,wkhc->wqhc", attention_b, value_heads, preferred_element_type=jnp.float32
    ).astype(jnp.bfloat16)
    weight_grad = jnp.einsum(
        "wqhc,wkhc->whqk", grad_heads, value_heads, preferred_element_type=jnp.float32
    )
    inner_sum = jnp.sum(attention * weight_grad, axis=-1, keepdims=True)
    score_grad = (attention * (weight_grad - inner_sum) * scaling).astype(jnp.bfloat16)
    query_grad = jnp.einsum(
        "whqk,wkhc->wqhc", score_grad, key_heads, preferred_element_type=jnp.float32
    ).astype(jnp.bfloat16)
    key_grad = jnp.einsum(
        "whqk,wqhc->wkhc", score_grad, query_heads, preferred_element_type=jnp.float32
    ).astype(jnp.bfloat16)
    value_grad = jnp.einsum(
        "whqk,wqhc->wkhc", attention_b, grad_heads, preferred_element_type=jnp.float32
    ).astype(jnp.bfloat16)
    shape_back = (count, members, width)
    return (
        mixed.reshape(shape_back),
        query_grad.reshape(shape_back),
        key_grad.reshape(shape_back),
        value_grad.reshape(shape_back),
    )


def body(tokens, grad_out, w_qkv, w_out):
    edges = tokens.shape[:3]
    width = tokens.shape[3]
    members = GRID**3
    token_flat = tokens.reshape(-1, width)
    grad_flat = grad_out.reshape(-1, width)
    qkv = jnp.dot(token_flat, w_qkv, preferred_element_type=jnp.float32).astype(jnp.bfloat16)
    grad_mixed = lax.dot_general(
        grad_flat, w_out, (((1,), (1,)), ((), ())), preferred_element_type=jnp.float32
    ).astype(jnp.bfloat16)
    payload = jnp.concatenate([qkv.reshape(-1, 3, width), grad_mixed.reshape(-1, 1, width)], axis=1)
    payload = payload.transpose(1, 0, 2).reshape((4,) + edges + (width,))
    windows = to_windows(payload)
    count = windows.shape[1]
    block = math.gcd(count, 16)
    rounds = count // block
    shaped = windows.reshape(4, rounds, block, members, width)

    def one_block(carry, pieces):
        mixed, query_grad, key_grad, value_grad = attend(pieces[0], pieces[1], pieces[2], pieces[3])
        return (carry, jnp.stack([query_grad, key_grad, value_grad, mixed]))

    unused, results = lax.scan(
        one_block, jnp.zeros((), jnp.float32), (shaped[0], shaped[1], shaped[2], shaped[3])
    )
    results = results.transpose(1, 0, 2, 3, 4).reshape(4, count, members, width)
    returned = from_windows(results, edges).reshape(4, -1, width)
    qkv_grad = returned[:3].transpose(1, 0, 2).reshape(-1, 3 * width)
    mixed_flat = returned[3]
    grad_tokens = (
        lax.dot_general(
            qkv_grad, w_qkv, (((1,), (1,)), ((), ())), preferred_element_type=jnp.float32
        )
        .astype(jnp.bfloat16)
        .reshape(tokens.shape)
    )
    part_qkv = lax.dot_general(
        token_flat, qkv_grad, (((0,), (0,)), ((), ())), preferred_element_type=jnp.float32
    )
    part_out = lax.dot_general(
        mixed_flat, grad_flat, (((0,), (0,)), ((), ())), preferred_element_type=jnp.float32
    )
    total_qkv, total_out = lax.psum((part_qkv, part_out), ("gx", "gy", "gz"))
    return (grad_tokens, total_qkv, total_out)


def solution(mesh):
    return jax.shard_map(
        body,
        mesh=mesh,
        in_specs=(P("gx", "gy", "gz", None), P("gx", "gy", "gz", None), P(), P()),
        out_specs=(P("gx", "gy", "gz", None), P(), P()),
        check_vma=False,
    )
```

profile of v0, /device:TPU:1, one launch (start us, length us, event | category | flops | bytes accessed | tf_op | source)
XLA Modules:
  0.0 790.2 jit_solution(8808189917296009913)
XLA Ops:
  8.8 5.5 convolution_convert_fusion.2
  14.3 8.7 %copy.60 = bf16[4096,3,256]{2,0,1:T(8,128)(2,1)} copy(bf16[4096,3,256]{0,2,1:T(8,128)(2,1)} %bitcast.120) | data formatting | bytes 12582912 | tf_op jit(solution)/shard_map/reshape | solution.py:111
  25.3 6.7 pad_maximum_fusion
  32.0 7.8 copy.61
  39.8 13.1 %copy.62 = bf16[128,4,4,4,2,256]{5,4,3,2,1,0:T(2,128)(2,1)} copy(bf16[128,4,4,4,2,256]{5,0,4,3,2,1:T(8,128)(2,1)} %bitcast.126) | data formatting | bytes 16777216 | tf_op jit(solution)/shard_map/reshape | solution.py:22
  52.9 12.0 %all-to-all-start = ((bf16[128,4,4,4,2,256]{5,4,3,2,1,0:T(2,128)(2,1)}), bf16[128,4,4,4,2,256]{5,4,3,2,1,0:T(2,128)(2,1)}, u32[]{:S(2)}, u32[]{:S(2)}) async-start(bf16[128,4,4,4,2,256]{5,4,3,2,1,0:T(2,128)(2,1)} %copy.62), calls=%async_computation | async-start | bytes 16777216 | tf_op jit(solution)/shard_map/all_to_all | solution.py:21
  65.1 98.8 %all-to-all-done = bf16[128,4,4,4,2,256]{5,4,3,2,1,0:T(2,128)(2,1)} async-done(((bf16[128,4,4,4,2,256]{5,4,3,2,1,0:T(2,128)(2,1)}), bf16[128,4,4,4,2,256]{5,4,3,2,1,0:T(2,128)(2,1)}, u32[]{:S(2)}, u32[]{:S(2)}) %all-to-all-start) | async-done | bytes 8388640 | tf_op jit(solution)/shard_map/all_to_all | solution.py:21
  163.9 9.2 %copy.63 = bf16[4,4,8,4,4,4,2,256]{7,5,6,2,1,4,0,3:T(4,128)(2,1)S(1)} copy(bf16[4,4,8,4,4,4,2,256]{7,6,5,4,3,2,1,0:T(2,128)(2,1)} %bitcast.21) | data formatting | bytes 16777216 | tf_op jit(solution)/shard_map/reshape | solution.py:28
  173.1 7.5 fusion.35
  192.4 227.2 %while.10 = (s32[]{:T(128)}, bf16[4,4,16,64,256]{3,4,2,1,0:T(8,128)(2,1)}, bf16[4,16,64,256]{3,0,2,1:T(4,128)(2,1)}, bf16[4,16,64,256]{3,0,2,1:T(4,128)(2,1)}, b...) while((s32[]{:T(128)}, bf16[4,4,16,64,256]{3,4,2,1,0:T(8,128)(2,1)}, ...), condition=%wide.region_4.5_spmd, body=%wide.region_0.4_spmd.sunk | while | flops 221790400 | bytes 56787708 | solution.py:123
  192.8 5.6 constant_dynamic-slice_fusion.7
  198.4 3.6 copy.94
  204.0 5.2 fusion.87
  209.2 5.6 constant_dynamic-slice_fusion.6
  220.4 4.4 fusion.88
  224.8 8.1 %fusion.90 = bf16[16,8,32,64]{3,2,1,0:T(8,128)(2,1)} fusion(bf16[16,64,8,32]{1,3,2,0:T(8,128)(2,1)S(1)} %bitcast.136, f32[16,8,64,64]{2,3,1,0:T(8,128)} %fusion.88, f32[16,8,64,64]{2,3,1,0:T(8,128)} %get-tuple-element.136, f32[16,8,64]{2,1,0:T(8,128)S(1)} %get-tuple-element.137), kind=kOutput, calls=%fused_computation.16.clone.1 | convolution fusion | flops 37494848 | bytes 5275648 | tf_op jit(solution)/shard_map/while/body/eval_jaxpr/whqk,wkhc->wqhc/dot_general | solution.py:83
  232.9 8.6 %fusion.89 = bf16[16,8,32,64]{3,2,1,0:T(8,128)(2,1)} fusion(bf16[16,64,8,32]{1,3,2,0:T(8,128)(2,1)} %bitcast.134, f32[16,8,64,64]{2,3,1,0:T(8,128)} %fusion.88, f32[16,8,64,64]{2,3,1,0:T(8,128)} %get-tuple-element.136, f32[16,8,64]{2,1,0:T(8,128)S(1)} %get-tuple-element.137), kind=kOutput, calls=%fused_computation.17.clone.1 | convolution fusion | flops 37494848 | bytes 5275648 | tf_op jit(solution)/shard_map/while/body/eval_jaxpr/whqk,wqhc->wkhc/dot_general | solution.py:86
  249.4 5.6 constant_dynamic-slice_fusion.7
  255.0 3.6 copy.94
  260.6 5.2 fusion.87
  265.8 5.6 constant_dynamic-slice_fusion.6
  277.1 4.4 fusion.88
  281.4 8.1 %fusion.90 = bf16[16,8,32,64]{3,2,1,0:T(8,128)(2,1)} fusion(bf16[16,64,8,32]{1,3,2,0:T(8,128)(2,1)S(1)} %bitcast.136, f32[16,8,64,64]{2,3,1,0:T(8,128)} %fusion.88, f32[16,8,64,64]{2,3,1,0:T(8,128)} %get-tuple-element.136, f32[16,8,64]{2,1,0:T(8,128)S(1)} %get-tuple-element.137), kind=kOutput, calls=%fused_computation.16.clone.1 | convolution fusion | flops 37494848 | bytes 5275648 | tf_op jit(solution)/shard_map/while/body/eval_jaxpr/whqk,wkhc->wqhc/dot_general | solution.py:83
  289.6 8.6 %fusion.89 = bf16[16,8,32,64]{3,2,1,0:T(8,128)(2,1)} fusion(bf16[16,64,8,32]{1,3,2,0:T(8,128)(2,1)} %bitcast.134, f32[16,8,64,64]{2,3,1,0:T(8,128)} %fusion.88, f32[16,8,64,64]{2,3,1,0:T(8,128)} %get-tuple-element.136, f32[16,8,64]{2,1,0:T(8,128)S(1)} %get-tuple-element.137), kind=kOutput, calls=%fused_computation.17.clone.1 | convolution fusion | flops 37494848 | bytes 5275648 | tf_op jit(solution)/shard_map/while/body/eval_jaxpr/whqk,wqhc->wkhc/dot_general | solution.py:86
  306.1 5.6 constant_dynamic-slice_fusion.7
  311.7 3.6 copy.94
  317.3 5.2 fusion.87
  322.6 5.6 constant_dynamic-slice_fusion.6
  333.8 4.4 fusion.88
  338.1 8.1 %fusion.90 = bf16[16,8,32,64]{3,2,1,0:T(8,128)(2,1)} fusion(bf16[16,64,8,32]{1,3,2,0:T(8,128)(2,1)S(1)} %bitcast.136, f32[16,8,64,64]{2,3,1,0:T(8,128)} %fusion.88, f32[16,8,64,64]{2,3,1,0:T(8,128)} %get-tuple-element.136, f32[16,8,64]{2,1,0:T(8,128)S(1)} %get-tuple-element.137), kind=kOutput, calls=%fused_computation.16.clone.1 | convolution fusion | flops 37494848 | bytes 5275648 | tf_op jit(solution)/shard_map/while/body/eval_jaxpr/whqk,wkhc->wqhc/dot_general | solution.py:83
  346.3 8.6 %fusion.89 = bf16[16,8,32,64]{3,2,1,0:T(8,128)(2,1)} fusion(bf16[16,64,8,32]{1,3,2,0:T(8,128)(2,1)} %bitcast.134, f32[16,8,64,64]{2,3,1,0:T(8,128)} %fusion.88, f32[16,8,64,64]{2,3,1,0:T(8,128)} %get-tuple-element.136, f32[16,8,64]{2,1,0:T(8,128)S(1)} %get-tuple-element.137), kind=kOutput, calls=%fused_computation.17.clone.1 | convolution fusion | flops 37494848 | bytes 5275648 | tf_op jit(solution)/shard_map/while/body/eval_jaxpr/whqk,wqhc->wkhc/dot_general | solution.py:86
  362.8 5.6 constant_dynamic-slice_fusion.7
  368.4 3.6 copy.94
  374.0 5.2 fusion.87
  379.2 5.6 constant_dynamic-slice_fusion.6
  390.5 4.4 fusion.88
  394.8 8.1 %fusion.90 = bf16[16,8,32,64]{3,2,1,0:T(8,128)(2,1)} fusion(bf16[16,64,8,32]{1,3,2,0:T(8,128)(2,1)S(1)} %bitcast.136, f32[16,8,64,64]{2,3,1,0:T(8,128)} %fusion.88, f32[16,8,64,64]{2,3,1,0:T(8,128)} %get-tuple-element.136, f32[16,8,64]{2,1,0:T(8,128)S(1)} %get-tuple-element.137), kind=kOutput, calls=%fused_computation.16.clone.1 | convolution fusion | flops 37494848 | bytes 5275648 | tf_op jit(solution)/shard_map/while/body/eval_jaxpr/whqk,wkhc->wqhc/dot_general | solution.py:83
  403.0 8.6 %fusion.89 = bf16[16,8,32,64]{3,2,1,0:T(8,128)(2,1)} fusion(bf16[16,64,8,32]{1,3,2,0:T(8,128)(2,1)} %bitcast.134, f32[16,8,64,64]{2,3,1,0:T(8,128)} %fusion.88, f32[16,8,64,64]{2,3,1,0:T(8,128)} %get-tuple-element.136, f32[16,8,64]{2,1,0:T(8,128)S(1)} %get-tuple-element.137), kind=kOutput, calls=%fused_computation.17.clone.1 | convolution fusion | flops 37494848 | bytes 5275648 | tf_op jit(solution)/shard_map/while/body/eval_jaxpr/whqk,wqhc->wkhc/dot_general | solution.py:86
  419.6 20.6 %copy.72 = bf16[4,4,16,64,256]{4,1,3,2,0:T(4,128)(2,1)} copy(bf16[4,4,16,64,256]{3,4,2,0,1:T(8,128)(2,1)} %bitcast.142) | data formatting | bytes 16777216 | tf_op jit(solution)/shard_map/transpose | solution.py:126
  440.2 11.1 %copy.73 = bf16[4,4,4,4,4,4,4,256]{7,4,6,5,3,2,1,0:T(4,128)(2,1)} copy(bf16[4,4,4,4,4,4,4,256]{7,2,5,3,1,6,4,0:T(4,128)(2,1)} %bitcast.121) | data formatting | bytes 16777216 | tf_op jit(solution)/shard_map/transpose | solution.py:45
  451.3 9.1 %copy.74 = bf16[4,4,8,4,4,4,2,256]{7,2,1,0,6,5,4,3:T(8,128)(2,1)} copy(bf16[4,4,8,4,4,4,2,256]{7,5,6,2,1,4,0,3:T(4,128)(2,1)} %bitcast.127) | data formatting | bytes 16777216 | tf_op jit(solution)/shard_map/transpose | solution.py:49
  460.4 12.2 %copy.75 = bf16[128,4,4,4,2,256]{5,4,3,2,1,0:T(2,128)(2,1)S(1)} copy(bf16[128,4,4,4,2,256]{5,0,4,3,2,1:T(8,128)(2,1)} %bitcast.128) | data formatting | bytes 16777216 | tf_op jit(solution)/shard_map/reshape | solution.py:51
  472.7 117.0 %all_to_all.10 = bf16[128,4,4,4,2,256]{5,4,3,2,1,0:T(2,128)(2,1)} all-to-all(bf16[128,4,4,4,2,256]{5,4,3,2,1,0:T(2,128)(2,1)S(1)} %copy.75), channel_id=1, replica_groups=mesh['gx'=4,'gy'=4,'gz'=8] {'gx','gy','gz'}, dimensions={0} | all-to-all | bytes 16777216 | tf_op jit(solution)/shard_map/all_to_all | solution.py:50
  589.7 15.8 %copy.76 = bf16[128,4,4,4,2,256]{5,0,4,3,2,1:T(8,128)(2,1)} copy(bf16[128,4,4,4,2,256]{5,4,3,2,1,0:T(2,128)(2,1)} %all_to_all.10) | data formatting | bytes 16777216 | tf_op jit(solution)/shard_map/all_to_all | solution.py:50
  615.5 9.0 %copy.78 = bf16[4096,3,256]{0,2,1:T(8,128)(2,1)} copy(bf16[4096,3,256]{2,0,1:T(8,128)(2,1)} %bitcast.141) | data formatting | bytes 12582912 | tf_op jit(solution)/shard_map/transpose | solution.py:128
  624.5 5.6 convolution_bitcast_fusion
  633.2 6.0 convolution_convert_fusion.4
  639.2 140.1 %all-reduce.3.cloned.1.call-done = (f32[256,768]{0,1:T(8,128)}, f32[256,256]{1,0:T(8,128)}) async-done(((f32[256,768]{0,1:T(8,128)}, f32[256,256]{1,0:T(8,128)}), (f32[256,768]{0,1:T(8,128)}, f32[256,256]{1,0:T(8,128)})) %all-reduce.3.cloned.1.call-update) | async-done | bytes 1048592 | tf_op jit(solution)/shard_map/psum | solution.py:143
  (97 shorter events, 94.4 us)
Async XLA Ops:
  7.2 1.6 copy-start
  14.3 8.7 %copy-start.9 = (bf16[256,256]{1,0:T(8,128)(2,1)S(1)}, bf16[256,256]{1,0:T(8,128)(2,1)}, u32[]{:S(2)}) copy-start(bf16[256,256]{1,0:T(8,128)(2,1)} %param.9) | copy-start | bytes 393220
  52.9 111.0 %all-to-all-start = ((bf16[128,4,4,4,2,256]{5,4,3,2,1,0:T(2,128)(2,1)}), bf16[128,4,4,4,2,256]{5,4,3,2,1,0:T(2,128)(2,1)}, u32[]{:S(2)}, u32[]{:S(2)}) async-start(bf16[128,4,4,4,2,256]{5,4,3,2,1,0:T(2,128)(2,1)} %copy.62), calls=%async_computation | async-start | bytes 16777216 | tf_op jit(solution)/shard_map/all_to_all | solution.py:21
  64.9 714.3 %all-reduce.3.cloned.1.call-start = ((), (), s32[]{:S(2)}) async-start(), calls=%async_computation.2 | async-start | bytes 2097152 | tf_op jit(solution)/shard_map/psum | solution.py:143
  220.4 4.4 copy-start.5
  232.9 8.7 %copy-start.2 = (bf16[1,16,64,256]{2,3,1,0:T(8,128)(2,1)S(1)}, bf16[1,16,64,256]{2,3,1,0:T(8,128)(2,1)}, u32[]{:S(2)}) copy-start(bf16[1,16,64,256]{2,3,1,0:T(8,128)(2,1)} %copy.96) | copy-start | bytes 1572868 | tf_op jit(solution)/shard_map/while
  241.6 3.5 copy-start.1
  241.6 3.8 copy-start.10
  245.4 1.2 copy-start.3
  245.4 1.5 copy-start.4
  277.0 4.4 copy-start.5
  289.6 8.7 %copy-start.2 = (bf16[1,16,64,256]{2,3,1,0:T(8,128)(2,1)S(1)}, bf16[1,16,64,256]{2,3,1,0:T(8,128)(2,1)}, u32[]{:S(2)}) copy-start(bf16[1,16,64,256]{2,3,1,0:T(8,128)(2,1)} %copy.96) | copy-start | bytes 1572868 | tf_op jit(solution)/shard_map/while
  298.2 3.5 copy-start.1
  298.2 3.8 copy-start.10
  302.0 1.2 copy-start.3
  302.0 1.5 copy-start.4
  333.8 4.4 copy-start.5
  346.3 8.7 %copy-start.2 = (bf16[1,16,64,256]{2,3,1,0:T(8,128)(2,1)S(1)}, bf16[1,16,64,256]{2,3,1,0:T(8,128)(2,1)}, u32[]{:S(2)}) copy-start(bf16[1,16,64,256]{2,3,1,0:T(8,128)(2,1)} %copy.96) | copy-start | bytes 1572868 | tf_op jit(solution)/shard_map/while
  354.9 3.5 copy-start.1
  354.9 3.8 copy-start.10
  358.7 1.2 copy-start.3
  358.7 1.5 copy-start.4
  390.5 4.4 copy-start.5
  403.0 8.7 %copy-start.2 = (bf16[1,16,64,256]{2,3,1,0:T(8,128)(2,1)S(1)}, bf16[1,16,64,256]{2,3,1,0:T(8,128)(2,1)}, u32[]{:S(2)}) copy-start(bf16[1,16,64,256]{2,3,1,0:T(8,128)(2,1)} %copy.96) | copy-start | bytes 1572868 | tf_op jit(solution)/shard_map/while
  411.6 3.5 copy-start.1
  411.6 3.8 copy-start.10
  415.4 1.2 copy-start.3
  415.4 1.5 copy-start.4
  624.5 5.6 copy-start.6
  630.1 1.6 copy-start.7
  630.3 2.9 copy-start.8
Sparse Core Ops, SparseCore 0:
  633.3 145.8 all-reduce.2
where the time goes:
time: 797 us; the launch traced here: 790 us
  local copies, waits for them, and re-layouts  247 us (31%)
  waiting for transfers between devices  239 us (30%)
  matrix products  143 us (18%)
  blocking collectives  117 us (15%)
  other arithmetic  16.9 us (2%)
  between operations  14.4 us (2%)
  starting transfers between devices  12.2 us (2%)
    psum x1, waiting for transfers between devices, body(): total_qkv, total_out = lax.psum((part_qkv, part_out), ('gx', 'gy', 'gz'))  140 us
    all_to_all x1, blocking collectives, from_windows(): lax.all_to_all(arranged.reshape((size_x * size_y * size_z,) + inner), ('g...  117 us
    all_to_all x1, waiting for transfers between devices, to_windows(): lax.all_to_all(arranged.reshape((size_x * size_y * size_z,) + inner), ('g...  98.8 us
    dynamic_slice x24, local copies, waits for them, and re-layouts, body(): lax.scan(one_block, jnp.zeros((), jnp.float32), (shaped[0], shaped[1], sh...  89.8 us
    dot_general x4, matrix products, attend(): jnp.einsum('whqk,wqhc->wkhc', score_grad, query_heads, preferred_element_...  34.6 us
    dot_general x4, matrix products, attend(): jnp.einsum('whqk,wkhc->wqhc', score_grad, key_heads, preferred_element_ty...  32.5 us
    sub x4, matrix products, attend(): attention = jax.nn.softmax(scores, axis=-1)  20.9 us
    transpose x1, local copies, waits for them, and re-layouts, body(): results = results.transpose(1, 0, 2, 3, 4).reshape(4, count, members, width)  20.6 us
  transfers between devices with their start and end apart: 2, of which 2 were waited for; matrix products, arithmetic and copies ran while one was open for 1% of the time, Pallas kernels for 0%

commit v1 on v0

v1 whole, which is shorter than its diff:
```python
import functools
import math

import jax
import jax.numpy as jnp
from jax import lax
from jax.experimental import pallas as pl
from jax.experimental.pallas import tpu as pltpu
from jax.sharding import PartitionSpec as P

BF = jnp.bfloat16
F32 = jnp.float32
MESH = pl.DeviceIdType.MESH
HD = 32
MEM = 64
WIN = 16
PARTS = 4
D = 256
NN = (((1,), (0,)), ((), ()))
NT = (((1,), (1,)), ((), ()))
TN = (((0,), (0,)), ((), ()))
SCALE = HD ** -0.5


def dot(a, b, dims=NN):
    return lax.dot_general(a, b, dims, preferred_element_type=F32)


def swap_matrix():
    row = lax.broadcasted_iota(jnp.int32, (256, 256), 0)
    col = lax.broadcasted_iota(jnp.int32, (256, 256), 1)
    return jnp.where((row % 16) * 16 + row // 16 == col, 1.0, 0.0).astype(BF)


def spread(rows):
    lane = lax.broadcasted_iota(jnp.int32, (MEM, 128), 1) // HD
    return jnp.concatenate([jnp.where(lane == h, rows, jnp.zeros_like(rows)) for h in range(4)], axis=0)


def gather_heads(wide):
    lane = lax.broadcasted_iota(jnp.int32, (MEM, 128), 1) // HD
    out = wide[3 * MEM:]
    for h in (2, 1, 0):
        out = jnp.where(lane == h, wide[h * MEM:(h + 1) * MEM], out)
    return out


def columns(hg):
    return [slice(b * D + hg * 128, b * D + hg * 128 + 128) for b in range(4)]


def stage1(w, qkvg, sbuf):
    for hg in range(2):
        q, k, v, g = (qkvg[w, :, s] for s in columns(hg))
        sbuf[0, hg] = dot(k, spread(q), NT)
        sbuf[1, hg] = dot(v, spread(g), NT)


def stage2(sbuf, pbuf):
    for hg in range(2):
        scores = sbuf[0, hg]
        top = jnp.max(scores, axis=0, keepdims=True)
        e = jnp.exp2((scores - top) * (SCALE * math.log2(math.e)))
        total = jnp.sum(e, axis=0, keepdims=True)
        att = e * (1.0 / total)
        wg = sbuf[1, hg]
        inner = jnp.sum(att * wg, axis=0, keepdims=True)
        pbuf[0, hg] = att.astype(BF)
        pbuf[1, hg] = (att * ((wg - inner) * SCALE)).astype(BF)


def stage3(w, qkvg, pbuf, mix, grads):
    for hg in range(2):
        s = columns(hg)
        q, k, v, g = (qkvg[w, :, part] for part in s)
        ab, sg = pbuf[0, hg], pbuf[1, hg]
        grads[w, :, s[2]] = dot(ab, spread(g)).astype(BF)
        grads[w, :, s[1]] = dot(sg, spread(q)).astype(BF)
        mix[w, :, s[0]] = gather_heads(dot(ab, v, TN)).astype(BF)
        grads[w, :, s[0]] = gather_heads(dot(sg, k, TN)).astype(BF)


def compute_part(arrived, leaving, swap, wqkv, wout, xw, gw, qkvg, grads, mix, dx, sbuf, pbuf, acc):
    for m in range(0, MEM, 16):
        rows = dot(swap, arrived[m:m + 16].reshape(256, 512)).astype(BF).reshape(WIN, 16, 512)
        xw[:, m:m + 16, :] = rows[:, :, :D]
        gw[:, m:m + 16, :] = rows[:, :, D:]

    x = xw[...].reshape(-1, D)
    g = gw[...].reshape(-1, D)
    qkvg[:, :, 0:3 * D] = dot(x, wqkv[...]).astype(BF).reshape(WIN, MEM, 3 * D)
    qkvg[:, :, 3 * D:] = dot(g, wout[...], NT).astype(BF).reshape(WIN, MEM, D)

    def step(i, carry):
        stage3(jnp.maximum(i - 2, 0), qkvg, pbuf, mix, grads)
        stage2(sbuf, pbuf)
        stage1(jnp.minimum(i, WIN - 1), qkvg, sbuf)
        return carry

    lax.fori_loop(0, WIN + 2, step, 0)

    gr = grads[...].reshape(-1, 3 * D)
    dx[...] = dot(gr, wqkv[...], NT).astype(BF).reshape(WIN, MEM, D)
    acc[:, 0:3 * D] += dot(xw[...].reshape(-1, D), gr, TN)
    acc[:, 3 * D:] += dot(mix[...].reshape(-1, D), gw[...].reshape(-1, D), TN)

    for m in range(0, MEM, 16):
        rows = dx[:, m:m + 16, :].reshape(256, D)
        leaving[m:m + 16] = dot(swap, rows).astype(BF).reshape(16, WIN, D)


def kernel(tok, grd, wqkv, wout, out, dwqkv, dwout, staged, arrived, leaving, swap, xw, gw, qkvg, grads, mix, dx, sbuf, pbuf,
           acc, accb, terms, half, pair, sums, gathered, stage_sem, go_sem, come_sem, back_sem, land_sem, dw_sem):
    y, gy, gz = lax.axis_index("gx"), lax.axis_index("gy"), lax.axis_index("gz")
    x_hi, core = gy // 2, gy % 2
    x, z_hi, z_lo = x_hi * 2 + gz // 4, gz % 4 // 2, gz % 2
    me = y * 16 + x * 4 + z_hi * 2 + core

    def place(y_of, x_of, z_of, core_of):
        return {"gx": y_of, "gy": x_of // 2 * 2 + core_of, "gz": x_of % 2 * 4 + z_of * 2 + 1 - z_lo}

    def peer(j):
        j0, j1, j2 = j % 4, j // 4 % 4, j // 16
        x_of = (x + j0) % 4
        y_of = (y + j0 + j1) % 4
        e = (j0 + j1 + j2) % 4
        z_of, core_of = (z_hi + e) % 2, (core + e // 2) % 2
        return y_of * 16 + x_of * 4 + z_of * 2 + core_of, place(y_of, x_of, z_of, core_of)

    def for_peers(act):
        def one(j, carry):
            act(*peer(j))
            return carry
        lax.fori_loop(0, MEM, one, 0)

    def wait(ref, sem):
        pltpu.make_async_copy(ref, ref, sem).wait()

    stagings = []
    for c in range(PARTS):
        for k, ref in enumerate((tok, grd)):
            copy = pltpu.make_async_copy(ref.at[:, c], staged.at[c, :, :, pl.ds(k * D, D)], stage_sem.at[c, k])
            copy.start()
            stagings.append(copy)

    barrier = pltpu.get_barrier_semaphore()
    for_peers(lambda t, device: pl.semaphore_signal(barrier, inc=1, device_id=device, device_id_type=MESH))
    swap[...] = swap_matrix()
    acc[...] = jnp.zeros_like(acc)
    pl.semaphore_wait(barrier, MEM)

    for c in range(PARTS):
        stagings[2 * c].wait()
        stagings[2 * c + 1].wait()
        for_peers(lambda t, device: pltpu.make_async_remote_copy(
            staged.at[c, t], arrived.at[c, me], go_sem.at[c], come_sem.at[c], device_id=device, device_id_type=MESH).start())

    def part(c, carry):
        wait(arrived.at[c], come_sem.at[c])
        compute_part(arrived.at[c], leaving.at[c], swap[...], wqkv, wout, xw, gw, qkvg, grads, mix, dx, sbuf, pbuf, acc)
        for_peers(lambda t, device: pltpu.make_async_remote_copy(
            leaving.at[c, t], out.at[me, c], back_sem, land_sem, device_id=device, device_id_type=MESH).start())
        return carry

    lax.fori_loop(0, PARTS, part, 0)

    for s in range(MEM):
        accb[s] = acc[s // 4 * 16:s // 4 * 16 + 16, s % 4 * D:s % 4 * D + D].astype(BF)
    for_peers(lambda t, device: pltpu.make_async_remote_copy(
        accb.at[t], terms.at[me], dw_sem.at[0], dw_sem.at[1], device_id=device, device_id_type=MESH).start())
    wait(terms, dw_sem.at[1])
    total = terms[0].astype(F32)
    for s in range(1, MEM):
        total += terms[s].astype(F32)
    half[...] = total
    exchange = pltpu.make_async_remote_copy(
        half, pair, dw_sem.at[2], dw_sem.at[3], device_id=place(y, x, z_hi, core), device_id_type=MESH)
    exchange.start()
    exchange.wait()
    sums[...] = (half[...] + pair[...]).astype(BF)
    for_peers(lambda t, device: pltpu.make_async_remote_copy(
        sums, gathered.at[me], dw_sem.at[4], dw_sem.at[5], device_id=device, device_id_type=MESH).start())
    wait(gathered, dw_sem.at[5])
    for s in range(MEM):
        rows, column = slice(s // 4 * 16, s // 4 * 16 + 16), s % 4
        if column < 3:
            dwqkv[rows, column * D:column * D + D] = gathered[s].astype(F32)
        else:
            dwout[rows, :] = gathered[s].astype(F32)

    for c in range(PARTS):
        wait(staged.at[c], go_sem.at[c])
    wait(leaving, back_sem)
    wait(leaving, land_sem)
    wait(accb, dw_sem.at[0])
    wait(gathered, dw_sem.at[4])


def body(tokens, grad_out, w_qkv, w_out):
    shape = (MEM, PARTS, WIN, D)
    anywhere, vmem = pl.BlockSpec(memory_space=pl.ANY), pl.BlockSpec(memory_space=pltpu.VMEM)
    out, dwqkv, dwout = pl.pallas_call(
        kernel,
        out_shape=(jax.ShapeDtypeStruct(shape, BF), jax.ShapeDtypeStruct((D, 3 * D), F32), jax.ShapeDtypeStruct((D, D), F32)),
        in_specs=[anywhere, anywhere, vmem, vmem],
        out_specs=(anywhere, vmem, vmem),
        scratch_shapes=[
            pltpu.VMEM((PARTS, MEM, WIN, 2 * D), BF),
            pltpu.VMEM((PARTS, MEM, WIN, 2 * D), BF),
            pltpu.VMEM((PARTS, MEM, WIN, D), BF),
            pltpu.VMEM((256, 256), BF),
            pltpu.VMEM((WIN, MEM, D), BF),
            pltpu.VMEM((WIN, MEM, D), BF),
            pltpu.VMEM((WIN, MEM, 4 * D), BF),
            pltpu.VMEM((WIN, MEM, 3 * D), BF),
            pltpu.VMEM((WIN, MEM, D), BF),
            pltpu.VMEM((WIN, MEM, D), BF),
            pltpu.VMEM((2, 2, MEM, 256), F32),
            pltpu.VMEM((2, 2, MEM, 256), BF),
            pltpu.VMEM((D, 4 * D), F32),
            pltpu.VMEM((MEM, 16, D), BF),
            pltpu.VMEM((MEM, 16, D), BF),
            pltpu.VMEM((16, D), F32),
            pltpu.VMEM((16, D), F32),
            pltpu.VMEM((16, D), BF),
            pltpu.VMEM((MEM, 16, D), BF),
            pltpu.SemaphoreType.DMA((PARTS, 2)),
            pltpu.SemaphoreType.DMA((PARTS,)),
            pltpu.SemaphoreType.DMA((PARTS,)),
            pltpu.SemaphoreType.DMA(()),
            pltpu.SemaphoreType.DMA(()),
            pltpu.SemaphoreType.DMA((6,)),
        ],
        compiler_params=pltpu.CompilerParams(collective_id=0, has_side_effects=True, vmem_limit_bytes=48 << 20),
        name="grid_attention_backward",
    )(tokens.reshape(shape), grad_out.reshape(shape), w_qkv, w_out)
    return out.reshape(tokens.shape), dwqkv, dwout


def solution(mesh):
    spec = P("gx", "gy", "gz", None)
    return jax.shard_map(body, mesh=mesh, in_specs=(spec, spec, P(), P()), out_specs=(spec, P(), P()), check_vma=False)
```

time: 797 us -> 107 us (0.13)
  local copies, waits for them, and re-layouts: 247 us -> 6.39 us
  waiting for transfers between devices: 239 us -> 0 us
  matrix products: 143 us -> 0 us
  blocking collectives: 117 us -> 0 us
  Pallas kernels: 0 us -> 100 us
  other arithmetic: 16.9 us -> 0 us
  between operations: 14.4 us -> 0.65 us
  starting transfers between devices: 12.2 us -> 0 us
    psum x1 -> x0, waiting for transfers between devices: 140 us -> none  [body(): total_qkv, total_out = lax.psum((part_qkv, part_out), ('gx', 'gy', 'gz'))]
    dot_general x25 -> x0, matrix products: 122 us -> none  [the longest x4 34.6 us: attend(): jnp.einsum('whqk,wqhc->wkhc', score_grad, query_heads, preferred_element_...]
    all_to_all x1 -> x0, blocking collectives: 117 us -> none  [from_windows(): lax.all_to_all(arranged.reshape((size_x * size_y * size_z,) + inner), ('g...]
    pallas_call x0 -> x1, Pallas kernels: none -> 100 us  [body(): pl.pallas_call(kernel, out_shape=(jax.ShapeDtypeStruct(shape, BF), jax.Sh...]
    all_to_all x1 -> x0, waiting for transfers between devices: 98.8 us -> none  [to_windows(): lax.all_to_all(arranged.reshape((size_x * size_y * size_z,) + inner), ('g...]
    dynamic_slice x24 -> x0, local copies, waits for them, and re-layouts: 89.8 us -> none  [body(): lax.scan(one_block, jnp.zeros((), jnp.float32), (shaped[0], shaped[1], sh...]
    transpose x5 -> x0, local copies, waits for them, and re-layouts: 57.7 us -> none  [the longest x1 20.6 us: body(): results = results.transpose(1, 0, 2, 3, 4).reshape(4, count, members, width)]
    reshape x4 -> x0, local copies, waits for them, and re-layouts: 43.1 us -> none  [the longest x1 13.1 us: to_windows(): arranged.reshape((size_x * size_y * size_z,) + inner)]
  transfers between devices with their start and end apart: 2 -> 0, of which waited for: 2 -> 0; matrix products, arithmetic and copies ran while one was open for 1% -> 0% of each run, Pallas kernels for 0% -> 0%
where the time goes in v1:
time: 107 us
  Pallas kernels  100 us (93%)
  local copies, waits for them, and re-layouts  6.39 us (6%)
    pallas_call x1, Pallas kernels, body(): pl.pallas_call(kernel, out_shape=(jax.ShapeDtypeStruct(shape, BF), jax.Sh...  100 us
    unnamed x9, local copies, waits for them, and re-layouts  6.39 us

profile of v1, /device:TPU:1, one launch (start us, length us, event | category | flops | bytes accessed | tf_op | source)
XLA Modules:
  0.0 107.1 jit_solution(271332716574500134)
XLA Ops:
  0.6 0.0 copy-start
  0.6 1.6 %copy-done = bf16[16,16,16,256]{3,2,1,0:T(8,128)(2,1)S(1)} copy-done((bf16[16,16,16,256]{3,2,1,0:T(8,128)(2,1)S(1)}, bf16[16,16,16,256]{3,2,1,0:T(8,128)(2,1)}, u32[]{:S(2)}) %copy-start) | copy-done | bytes 2097176
  2.2 0.0 copy-start.1
  2.2 1.0 copy-done.1
  3.2 0.0 copy-start.2
  3.2 0.9 copy-done.2
  4.1 100.1 %grid_attention_backward.1 = (bf16[64,4,16,256]{3,2,1,0:T(8,128)(2,1)S(1)}, f32[256,768]{1,0:T(8,128)S(1)}, f32[256,256]{1,0:T(8,128)S(1)}) custom-call(bf16[64,4,16,256]{3,2,1,0:T(8,128)(2,1)S(1)} %bitcast.3, bf16[64,4,16,256]{3,2,1,0:T(8,128)(2,1)} %bitcast.5, bf16[256,768]{1,0:T(8,128)(2,1)S(1)} %copy-done.1, bf16[256,256]{1,0:T(8,128)(2,1)S(1)} %copy-done.2), custom_call_target="tpu_custom_call" | custom-call | tf_op jit(solution)/shard_map/grid_attention_backward/pallas_call | solution.py:202
  104.2 1.3 %copy.10 = bf16[16,16,16,256]{3,2,1,0:T(8,128)(2,1)} copy(bf16[16,16,16,256]{3,2,1,0:T(8,128)(2,1)S(1)} %bitcast.4) | data formatting | bytes 4194304
  105.5 0.9 copy.11
  106.4 0.7 copy.12
Async XLA Ops:
  0.6 1.6 %copy-start = (bf16[16,16,16,256]{3,2,1,0:T(8,128)(2,1)S(1)}, bf16[16,16,16,256]{3,2,1,0:T(8,128)(2,1)}, u32[]{:S(2)}) copy-start(bf16[16,16,16,256]{3,2,1,0:T(8,128)(2,1)} %param.4) | copy-start | bytes 6291460
  2.2 1.0 copy-start.1
  3.2 0.9 copy-start.2

commit v2 on v1

v2 whole, which is shorter than its diff:
```python
import functools
import math

import jax
import jax.numpy as jnp
from jax import lax
from jax.experimental import pallas as pl
from jax.experimental.pallas import tpu as pltpu
from jax.sharding import PartitionSpec as P

BF = jnp.bfloat16
F32 = jnp.float32
LOGICAL = pl.DeviceIdType.LOGICAL
HD = 32
MEM = 64
WIN = 16
PARTS = 4
STEP = 2
CHIPS = 32
D = 256
NN = (((1,), (0,)), ((), ()))
NT = (((1,), (1,)), ((), ()))
TN = (((0,), (0,)), ((), ()))
SCALE = HD ** -0.5


def dot(a, b, dims=NN):
    return lax.dot_general(a, b, dims, preferred_element_type=F32)


def swap_matrix():
    row = lax.broadcasted_iota(jnp.int32, (256, 256), 0)
    col = lax.broadcasted_iota(jnp.int32, (256, 256), 1)
    return jnp.where((row % 16) * 16 + row // 16 == col, 1.0, 0.0).astype(BF)


def spread(rows):
    lane = lax.broadcasted_iota(jnp.int32, (MEM, 128), 1) // HD
    return jnp.concatenate([jnp.where(lane == h, rows, jnp.zeros_like(rows)) for h in range(4)], axis=0)


def gather_heads(wide):
    lane = lax.broadcasted_iota(jnp.int32, (MEM, 128), 1) // HD
    out = wide[3 * MEM:]
    for h in (2, 1, 0):
        out = jnp.where(lane == h, wide[h * MEM:(h + 1) * MEM], out)
    return out


def columns(hg):
    return [slice(b * D + hg * 128, b * D + hg * 128 + 128) for b in range(4)]


def stage1(w, qkvg, sbuf):
    for hg in range(2):
        q, k, v, g = (qkvg[w, :, s] for s in columns(hg))
        sbuf[0, hg] = dot(k, spread(q), NT)
        sbuf[1, hg] = dot(v, spread(g), NT)


def stage2(sbuf, pbuf):
    for hg in range(2):
        scores = sbuf[0, hg]
        top = jnp.max(scores, axis=0, keepdims=True)
        e = jnp.exp2((scores - top) * (SCALE * math.log2(math.e)))
        total = jnp.sum(e, axis=0, keepdims=True)
        att = e * (1.0 / total)
        wg = sbuf[1, hg]
        inner = jnp.sum(att * wg, axis=0, keepdims=True)
        pbuf[hg, :MEM] = att.astype(BF)
        pbuf[hg, MEM:] = (att * ((wg - inner) * SCALE)).astype(BF)


def stage3(w, qkvg, pbuf, mix, grads):
    for hg in range(2):
        s = columns(hg)
        q, k, v, g = (qkvg[w, :, part] for part in s)
        both = pbuf[hg]
        rows = dot(both, jnp.concatenate([spread(g), spread(q)], axis=1))
        grads[w, :, s[2]] = rows[:MEM, :128].astype(BF)
        grads[w, :, s[1]] = rows[MEM:, 128:].astype(BF)
        zero = jnp.zeros_like(v)
        vk = jnp.concatenate([jnp.concatenate([v, zero], axis=1), jnp.concatenate([zero, k], axis=1)], axis=0)
        wide = dot(both, vk, TN)
        mix[w, :, s[0]] = gather_heads(wide[:, :128]).astype(BF)
        grads[w, :, s[0]] = gather_heads(wide[:, 128:]).astype(BF)


def attend(arrived, swap, wqkv, wout, xw, gw, qkvg, grads, mix, sbuf, pbuf, acc):
    for m in range(0, MEM, 16):
        rows = dot(swap[...], arrived[m:m + 16].reshape(256, 512)).astype(BF).reshape(WIN, 16, 512)
        xw[:, m:m + 16, :] = rows[:, :, :D]
        gw[:, m:m + 16, :] = rows[:, :, D:]

    x = xw[...].reshape(-1, D)
    g = gw[...].reshape(-1, D)
    qkvg[:, :, 0:3 * D] = dot(x, wqkv[...]).astype(BF).reshape(WIN, MEM, 3 * D)
    qkvg[:, :, 3 * D:] = dot(g, wout[...], NT).astype(BF).reshape(WIN, MEM, D)

    last = WIN // STEP - 1

    def step(i, carry):
        for u in range(STEP):
            stage3(jnp.maximum(i - 2, 0) * STEP + u, qkvg, pbuf.at[u], mix, grads)
        for u in range(STEP):
            stage2(sbuf.at[u], pbuf.at[u])
        for u in range(STEP):
            stage1(jnp.minimum(i, last) * STEP + u, qkvg, sbuf.at[u])
        return carry

    lax.fori_loop(0, last + 3, step, 0)

    acc[:, 0:3 * D] += dot(xw[...].reshape(-1, D), grads[...].reshape(-1, 3 * D), TN)
    acc[:, 3 * D:] += dot(mix[...].reshape(-1, D), gw[...].reshape(-1, D), TN)


def token_gradients(leaving, swap, wqkv, grads, dx):
    dx[...] = dot(grads[...].reshape(-1, 3 * D), wqkv[...], NT).astype(BF).reshape(WIN, MEM, D)
    for m in range(0, MEM, 16):
        rows = dx[:, m:m + 16, :].reshape(256, D)
        leaving[m:m + 16] = dot(swap[...], rows).astype(BF).reshape(16, WIN, D)


def kernel(tok, grd, wqkv_hbm, wout_hbm, out, dwqkv, dwout, staged, arrived, leaving, wqkv, wout, swap, xw, gw, qkvg, grads,
           mix, dx, sbuf, pbuf, acc, away, home, terms, half, pair, gathered,
           stage_sem, weight_sem, go_sem, come_sem, back_sem, land_sem, dw_sem):
    y, gy, gz = lax.axis_index("gx"), lax.axis_index("gy"), lax.axis_index("gz")
    x_hi, core = gy // 2, gy % 2
    x, z_hi, z_lo = x_hi * 2 + gz // 4, gz % 4 // 2, gz % 2
    chip = y * 8 + x * 2 + z_hi
    me = chip * 2 + core

    def device(y_of, x_of, z_of, core_of, z_low):
        return y_of * 32 + x_of // 2 * 16 + core_of * 8 + x_of % 2 * 4 + z_of * 2 + z_low

    ys = tuple((y + d) % 4 for d in range(4))
    xs = tuple((x + d) % 4 for d in range(4))
    ends = tuple(((z_hi + e) % 2, (core + e // 2) % 2) for e in range(4))
    y_part = tuple(v * 16 for v in ys)
    x_part = tuple((v * 4, device(0, v, 0, 0, 1 - z_lo)) for v in xs)
    end_part = tuple((z_of * 2 + core_of, device(0, 0, z_of, core_of, 0)) for z_of, core_of in ends)

    def for_partners(act):
        def outer(i, y_carry):
            def inner(k, e_carry):
                for d in range(4):
                    y_of, (x_num, x_dev), (e_num, e_dev) = y_carry[d], x_part[d], e_carry[d]
                    act(y_of + x_num + e_num, y_of * 2 + x_dev + e_dev)
                return e_carry[1:] + e_carry[:1]
            lax.fori_loop(0, 4, inner, end_part)
            return y_carry[1:] + y_carry[:1]
        lax.fori_loop(0, 4, outer, y_part)

    def for_chips(act):
        def outer(i, y_carry):
            for d in range(4):
                for z_of in (z_hi, 1 - z_hi):
                    y_of, (x_num, x_dev) = y_carry[d], x_part[d]
                    act((y_of + x_num) // 2 + z_of, y_of * 2 + x_dev + device(0, 0, z_of, core, 0))
            return y_carry[1:] + y_carry[:1]
        lax.fori_loop(0, 4, outer, y_part)

    other_core = device(y, x, z_hi, 1 - core, z_lo)
    across = device(y, x, z_hi, core, 1 - z_lo)

    def send(src, dst, send_sem, recv_sem, to):
        copy = pltpu.make_async_remote_copy(src, dst, send_sem, recv_sem, device_id=to, device_id_type=LOGICAL)
        copy.start()
        return copy

    def wait(ref, sem):
        pltpu.make_async_copy(ref, ref, sem).wait()

    stagings = []
    for c in range(PARTS):
        for k, ref in enumerate((tok, grd)):
            copy = pltpu.make_async_copy(ref.at[:, c], staged.at[c, :, :, pl.ds(k * D, D)], stage_sem.at[c, k])
            copy.start()
            stagings.append(copy)
    weights = [pltpu.make_async_copy(wqkv_hbm, wqkv, weight_sem.at[0]), pltpu.make_async_copy(wout_hbm, wout, weight_sem.at[1])]
    for copy in weights:
        copy.start()

    barrier = pltpu.get_barrier_semaphore()
    for_partners(lambda t, to: pl.semaphore_signal(barrier, inc=1, device_id=to, device_id_type=LOGICAL))
    pl.semaphore_signal(barrier, inc=1, device_id=other_core, device_id_type=LOGICAL)
    swap[...] = swap_matrix()
    acc[...] = jnp.zeros_like(acc)
    pl.semaphore_wait(barrier, MEM + 1)

    for c in range(PARTS):
        stagings[2 * c].wait()
        stagings[2 * c + 1].wait()
        for_partners(lambda t, to: send(staged.at[c, t], arrived.at[c, me], go_sem.at[c], come_sem.at[c], to))
    for copy in weights:
        copy.wait()

    rows = D // 2
    first, second = pl.ds(pl.multiple_of(core * rows, rows), rows), pl.ds(pl.multiple_of((1 - core) * rows, rows), rows)

    def part(c, carry):
        wait(arrived.at[c], come_sem.at[c])
        attend(arrived.at[c], swap, wqkv, wout, xw, gw, qkvg, grads, mix, sbuf, pbuf, acc)

        @pl.when(c == PARTS - 1)
        def _():
            away[0] = acc[second, :].astype(BF)
            send(away.at[0], away.at[1], dw_sem.at[0], dw_sem.at[1], other_core)

        token_gradients(leaving.at[c], swap, wqkv, grads, dx)

        @pl.when(c == PARTS - 1)
        def _():
            wait(away.at[1], dw_sem.at[1])
            both = (acc[first, :] + away[1].astype(F32)).astype(BF)
            for s in range(CHIPS):
                home[s] = both[s // 4 * 16:s // 4 * 16 + 16, s % 4 * D:s % 4 * D + D]
            for_chips(lambda t, to: send(home.at[t], terms.at[chip], dw_sem.at[2], dw_sem.at[3], to))

        for_partners(lambda t, to: send(leaving.at[c, t], out.at[me, c], back_sem, land_sem, to))
        return carry

    lax.fori_loop(0, PARTS, part, 0)

    wait(terms, dw_sem.at[3])
    total = terms[0].astype(F32)
    for s in range(1, CHIPS):
        total += terms[s].astype(F32)
    half[...] = total
    send(half, pair, dw_sem.at[4], dw_sem.at[5], across).wait()
    mine = home.at[CHIPS]
    mine[...] = (half[...] + pair[...]).astype(BF)
    for_chips(lambda t, to: send(mine, gathered.at[0, chip], dw_sem.at[6], dw_sem.at[7], to))
    wait(gathered.at[0], dw_sem.at[7])
    send(gathered.at[0], gathered.at[1], dw_sem.at[8], dw_sem.at[9], other_core)

    def write(owner, block):
        for s in range(CHIPS):
            where = pl.ds(pl.multiple_of(owner * rows + s // 4 * 16, 16), 16)
            if s % 4 < 3:
                dwqkv[where, s % 4 * D:s % 4 * D + D] = block[s].astype(F32)
            else:
                dwout[where, :] = block[s].astype(F32)

    write(core, gathered.at[0])
    wait(gathered.at[1], dw_sem.at[9])
    write(1 - core, gathered.at[1])

    for c in range(PARTS):
        wait(staged.at[c], go_sem.at[c])
    wait(leaving, back_sem)
    wait(leaving, land_sem)
    wait(away.at[0], dw_sem.at[0])
    wait(terms, dw_sem.at[2])
    wait(gathered.at[0], dw_sem.at[6])
    wait(gathered.at[0], dw_sem.at[8])


def body(tokens, grad_out, w_qkv, w_out):
    shape = (MEM, PARTS, WIN, D)
    hbm, anywhere, vmem = (pl.BlockSpec(memory_space=space) for space in (pltpu.HBM, pl.ANY, pltpu.VMEM))
    out, dwqkv, dwout = pl.pallas_call(
        kernel,
        out_shape=(jax.ShapeDtypeStruct(shape, BF), jax.ShapeDtypeStruct((D, 3 * D), F32), jax.ShapeDtypeStruct((D, D), F32)),
        in_specs=[hbm, hbm, hbm, hbm],
        out_specs=(anywhere, vmem, vmem),
        scratch_shapes=[
            pltpu.VMEM((PARTS, MEM, WIN, 2 * D), BF),
            pltpu.VMEM((PARTS, MEM, WIN, 2 * D), BF),
            pltpu.VMEM((PARTS, MEM, WIN, D), BF),
            pltpu.VMEM((D, 3 * D), BF),
            pltpu.VMEM((D, D), BF),
            pltpu.VMEM((256, 256), BF),
            pltpu.VMEM((WIN, MEM, D), BF),
            pltpu.VMEM((WIN, MEM, D), BF),
            pltpu.VMEM((WIN, MEM, 4 * D), BF),
            pltpu.VMEM((WIN, MEM, 3 * D), BF),
            pltpu.VMEM((WIN, MEM, D), BF),
            pltpu.VMEM((WIN, MEM, D), BF),
            pltpu.VMEM((STEP, 2, 2, MEM, 256), F32),
            pltpu.VMEM((STEP, 2, 2 * MEM, 256), BF),
            pltpu.VMEM((D, 4 * D), F32),
            pltpu.VMEM((2, D // 2, 4 * D), BF),
            pltpu.VMEM((CHIPS + 1, 16, D), BF),
            pltpu.VMEM((CHIPS, 16, D), BF),
            pltpu.VMEM((16, D), F32),
            pltpu.VMEM((16, D), F32),
            pltpu.VMEM((2, CHIPS, 16, D), BF),
            pltpu.SemaphoreType.DMA((PARTS, 2)),
            pltpu.SemaphoreType.DMA((2,)),
            pltpu.SemaphoreType.DMA((PARTS,)),
            pltpu.SemaphoreType.DMA((PARTS,)),
            pltpu.SemaphoreType.DMA(()),
            pltpu.SemaphoreType.DMA(()),
            pltpu.SemaphoreType.DMA((10,)),
        ],
        compiler_params=pltpu.CompilerParams(collective_id=0, has_side_effects=True, vmem_limit_bytes=48 << 20),
        name="grid_attention_backward",
    )(*(pltpu.with_memory_space_constraint(a, pltpu.HBM) for a in (tokens.reshape(shape), grad_out.reshape(shape), w_qkv, w_out)))
    return out.reshape(tokens.shape), dwqkv, dwout


def solution(mesh):
    spec = P("gx", "gy", "gz", None)
    return jax.shard_map(body, mesh=mesh, in_specs=(spec, spec, P(), P()), out_specs=(spec, P(), P()), check_vma=False)
```

time: 107 us -> 95.1 us (0.89)
  Pallas kernels: 100 us -> 91.4 us
  local copies, waits for them, and re-layouts: 6.39 us -> 2.9 us
    pallas_call x1, Pallas kernels: 100 us -> 91.4 us  [body(): pl.pallas_call(kernel, out_shape=(jax.ShapeDtypeStruct(shape, BF), jax.Sh...]
    unnamed x9 -> x3, local copies, waits for them, and re-layouts: 6.39 us -> 2.9 us
where the time goes in v2:
time: 95.1 us; the launch traced here: 95 us
  Pallas kernels  91.4 us (96%)
  local copies, waits for them, and re-layouts  2.9 us (3%)
    pallas_call x1, Pallas kernels, body(): pl.pallas_call(kernel, out_shape=(jax.ShapeDtypeStruct(shape, BF), jax.Sh...  91.4 us
    unnamed x3, local copies, waits for them, and re-layouts  2.9 us

profile of v2, /device:TPU:1, one launch (start us, length us, event | category | flops | bytes accessed | tf_op | source)
XLA Modules:
  0.0 95.0 jit_solution(8392911170412358178)
XLA Ops:
  0.6 91.4 %grid_attention_backward.1 = (bf16[64,4,16,256]{3,2,1,0:T(8,128)(2,1)S(1)}, f32[256,768]{1,0:T(8,128)S(1)}, f32[256,256]{1,0:T(8,128)S(1)}) custom-call(bf16[64,4,16,256]{3,2,1,0:T(8,128)(2,1)} %bitcast.4, bf16[64,4,16,256]{3,2,1,0:T(8,128)(2,1)} %bitcast.5, bf16[256,768]{1,0:T(8,128)(2,1)} %wqkv_hbm.1, bf16[256,256]{1,0:T(8,128)(2,1)} %wout_hbm.1), custom_call_target="tpu_custom_call" | custom-call | tf_op jit(solution)/shard_map/grid_attention_backward/pallas_call | solution.py:262
  92.1 1.3 %copy.10 = bf16[16,16,16,256]{3,2,1,0:T(8,128)(2,1)} copy(bf16[16,16,16,256]{3,2,1,0:T(8,128)(2,1)S(1)} %bitcast.3) | data formatting | bytes 4194304
  93.4 0.9 copy.11
  94.3 0.7 copy.12

commit v3 on v2

--- a/solution.py
+++ b/solution.py
@@ -140,7 +140,7 @@
     x_part = tuple((v * 4, device(0, v, 0, 0, 1 - z_lo)) for v in xs)
     end_part = tuple((z_of * 2 + core_of, device(0, 0, z_of, core_of, 0)) for z_of, core_of in ends)
 
-    def for_partners(act):
+    def for_partners(act, first=0, last=4):
         def outer(i, y_carry):
             def inner(k, e_carry):
                 for d in range(4):
@@ -149,7 +149,7 @@
                 return e_carry[1:] + e_carry[:1]
             lax.fori_loop(0, 4, inner, end_part)
             return y_carry[1:] + y_carry[:1]
-        lax.fori_loop(0, 4, outer, y_part)
+        lax.fori_loop(first, last, outer, y_part[first:] + y_part[:first])
 
     def for_chips(act):
         def outer(i, y_carry):
@@ -171,6 +171,9 @@
     def wait(ref, sem):
         pltpu.make_async_copy(ref, ref, sem).wait()
 
+    barrier = pltpu.get_barrier_semaphore()
+    for_partners(lambda t, to: pl.semaphore_signal(barrier, inc=1, device_id=to, device_id_type=LOGICAL))
+    pl.semaphore_signal(barrier, inc=1, device_id=other_core, device_id_type=LOGICAL)
     stagings = []
     for c in range(PARTS):
         for k, ref in enumerate((tok, grd)):
@@ -181,9 +184,6 @@
     for copy in weights:
         copy.start()
 
-    barrier = pltpu.get_barrier_semaphore()
-    for_partners(lambda t, to: pl.semaphore_signal(barrier, inc=1, device_id=to, device_id_type=LOGICAL))
-    pl.semaphore_signal(barrier, inc=1, device_id=other_core, device_id_type=LOGICAL)
     swap[...] = swap_matrix()
     acc[...] = jnp.zeros_like(acc)
     pl.semaphore_wait(barrier, MEM + 1)
@@ -195,6 +195,9 @@
     for copy in weights:
         copy.wait()
 
+    def send_back(c, first=0, last=4):
+        for_partners(lambda t, to: send(leaving.at[c, t], out.at[me, c], back_sem, land_sem, to), first, last)
+
     rows = D // 2
     first, second = pl.ds(pl.multiple_of(core * rows, rows), rows), pl.ds(pl.multiple_of((1 - core) * rows, rows), rows)
 
@@ -216,8 +219,22 @@
             for s in range(CHIPS):
                 home[s] = both[s // 4 * 16:s // 4 * 16 + 16, s % 4 * D:s % 4 * D + D]
             for_chips(lambda t, to: send(home.at[t], terms.at[chip], dw_sem.at[2], dw_sem.at[3], to))
-
-        for_partners(lambda t, to: send(leaving.at[c, t], out.at[me, c], back_sem, land_sem, to))
+            send_back(2, 2, 4)
+            send_back(3, 0, 1)
+
+        @pl.when(c == 0)
+        def _():
+            send_back(0, 0, 4)
+
+        @pl.when(c == 1)
+        def _():
+            send_back(1, 0, 3)
+
+        @pl.when(c == 2)
+        def _():
+            send_back(1, 3, 4)
+            send_back(2, 0, 2)
+
         return carry
 
     lax.fori_loop(0, PARTS, part, 0)
@@ -227,10 +244,13 @@
     for s in range(1, CHIPS):
         total += terms[s].astype(F32)
     half[...] = total
-    send(half, pair, dw_sem.at[4], dw_sem.at[5], across).wait()
+    exchange = send(half, pair, dw_sem.at[4], dw_sem.at[5], across)
+    send_back(3, 1, 2)
+    exchange.wait()
     mine = home.at[CHIPS]
     mine[...] = (half[...] + pair[...]).astype(BF)
     for_chips(lambda t, to: send(mine, gathered.at[0, chip], dw_sem.at[6], dw_sem.at[7], to))
+    send_back(3, 2, 4)
     wait(gathered.at[0], dw_sem.at[7])
     send(gathered.at[0], gathered.at[1], dw_sem.at[8], dw_sem.at[9], other_core)
 

time: 95.1 us -> 94.1 us (0.989)
    pallas_call x1, Pallas kernels: 91.4 us -> 90.5 us  [body(): pl.pallas_call(kernel, out_shape=(jax.ShapeDtypeStruct(shape, BF), jax.Sh...]
where the time goes in v3:
time: 94.1 us; the launch traced here: 94 us
  Pallas kernels  90.5 us (96%)
  local copies, waits for them, and re-layouts  2.9 us (3%)
    pallas_call x1, Pallas kernels, body(): pl.pallas_call(kernel, out_shape=(jax.ShapeDtypeStruct(shape, BF), jax.Sh...  90.5 us
    unnamed x3, local copies, waits for them, and re-layouts  2.9 us

profile of v3, /device:TPU:1, one launch (start us, length us, event | category | flops | bytes accessed | tf_op | source)
XLA Modules:
  0.0 94.0 jit_solution(10514613757747757503)
XLA Ops:
  0.6 90.5 %grid_attention_backward.1 = (bf16[64,4,16,256]{3,2,1,0:T(8,128)(2,1)S(1)}, f32[256,768]{1,0:T(8,128)S(1)}, f32[256,256]{1,0:T(8,128)S(1)}) custom-call(bf16[64,4,16,256]{3,2,1,0:T(8,128)(2,1)} %bitcast.4, bf16[64,4,16,256]{3,2,1,0:T(8,128)(2,1)} %bitcast.5, bf16[256,768]{1,0:T(8,128)(2,1)} %wqkv_hbm.1, bf16[256,256]{1,0:T(8,128)(2,1)} %wout_hbm.1), custom_call_target="tpu_custom_call" | custom-call | tf_op jit(solution)/shard_map/grid_attention_backward/pallas_call | solution.py:282
  91.1 1.3 %copy.10 = bf16[16,16,16,256]{3,2,1,0:T(8,128)(2,1)} copy(bf16[16,16,16,256]{3,2,1,0:T(8,128)(2,1)S(1)} %bitcast.3) | data formatting | bytes 4194304
  92.4 0.9 copy.11
  93.3 0.7 copy.12

commit v4 on v3

--- a/solution.py
+++ b/solution.py
@@ -141,15 +141,16 @@
     end_part = tuple((z_of * 2 + core_of, device(0, 0, z_of, core_of, 0)) for z_of, core_of in ends)
 
     def for_partners(act, first=0, last=4):
-        def outer(i, y_carry):
-            def inner(k, e_carry):
+        def outer(k, e_carry):
+            def inner(i, carry):
+                y_carry, e_now = carry
                 for d in range(4):
-                    y_of, (x_num, x_dev), (e_num, e_dev) = y_carry[d], x_part[d], e_carry[d]
+                    y_of, (x_num, x_dev), (e_num, e_dev) = y_carry[d], x_part[d], e_now[d]
                     act(y_of + x_num + e_num, y_of * 2 + x_dev + e_dev)
-                return e_carry[1:] + e_carry[:1]
-            lax.fori_loop(0, 4, inner, end_part)
-            return y_carry[1:] + y_carry[:1]
-        lax.fori_loop(first, last, outer, y_part[first:] + y_part[:first])
+                return y_carry[1:] + y_carry[:1], e_now[-1:] + e_now[:-1]
+            lax.fori_loop(0, 4, inner, (y_part, e_carry))
+            return e_carry[1:] + e_carry[:1]
+        lax.fori_loop(first, last, outer, end_part[first:] + end_part[:first])
 
     def for_chips(act):
         def outer(i, y_carry):

time: 94.1 us -> 93.5 us (level)
  no operation moved by 1% of the time
where the time goes in v4:
time: 93.5 us; the launch traced here: 93.3 us
  Pallas kernels  89.8 us (96%)
  local copies, waits for them, and re-layouts  2.9 us (3%)
    pallas_call x1, Pallas kernels, body(): pl.pallas_call(kernel, out_shape=(jax.ShapeDtypeStruct(shape, BF), jax.Sh...  89.8 us
    unnamed x3, local copies, waits for them, and re-layouts  2.9 us

profile of v4, /device:TPU:1, one launch (start us, length us, event | category | flops | bytes accessed | tf_op | source)
XLA Modules:
  0.0 93.3 jit_solution(13105727452177601292)
XLA Ops:
  0.6 89.8 %grid_attention_backward.1 = (bf16[64,4,16,256]{3,2,1,0:T(8,128)(2,1)S(1)}, f32[256,768]{1,0:T(8,128)S(1)}, f32[256,256]{1,0:T(8,128)S(1)}) custom-call(bf16[64,4,16,256]{3,2,1,0:T(8,128)(2,1)} %bitcast.4, bf16[64,4,16,256]{3,2,1,0:T(8,128)(2,1)} %bitcast.5, bf16[256,768]{1,0:T(8,128)(2,1)} %wqkv_hbm.1, bf16[256,256]{1,0:T(8,128)(2,1)} %wout_hbm.1), custom_call_target="tpu_custom_call" | custom-call | tf_op jit(solution)/shard_map/grid_attention_backward/pallas_call | solution.py:283
  90.4 1.3 %copy.10 = bf16[16,16,16,256]{3,2,1,0:T(8,128)(2,1)} copy(bf16[16,16,16,256]{3,2,1,0:T(8,128)(2,1)S(1)} %bitcast.3) | data formatting | bytes 4194304
  91.8 0.9 copy.11
  92.6 0.7 copy.12

commit v5 on v4

--- a/solution.py
+++ b/solution.py
@@ -121,8 +121,8 @@
         leaving[m:m + 16] = dot(swap[...], rows).astype(BF).reshape(16, WIN, D)
 
 
-def kernel(tok, grd, wqkv_hbm, wout_hbm, out, dwqkv, dwout, staged, arrived, leaving, wqkv, wout, swap, xw, gw, qkvg, grads,
-           mix, dx, sbuf, pbuf, acc, away, home, terms, half, pair, gathered,
+def kernel(tok, grd, wqkv_hbm, wout_hbm, out, gathered, staged, arrived, leaving, wqkv, wout, swap, xw, gw, qkvg, grads,
+           mix, dx, sbuf, pbuf, acc, away, home, terms, half, pair,
            stage_sem, weight_sem, go_sem, come_sem, back_sem, land_sem, dw_sem):
     y, gy, gz = lax.axis_index("gx"), lax.axis_index("gy"), lax.axis_index("gz")
     x_hi, core = gy // 2, gy % 2
@@ -154,7 +154,7 @@
 
     def for_chips(act):
         def outer(i, y_carry):
-            for d in range(4):
+            for d in (2, 1, 3, 0):
                 for z_of in (z_hi, 1 - z_hi):
                     y_of, (x_num, x_dev) = y_carry[d], x_part[d]
                     act((y_of + x_num) // 2 + z_of, y_of * 2 + x_dev + device(0, 0, z_of, core, 0))
@@ -248,24 +248,13 @@
     exchange = send(half, pair, dw_sem.at[4], dw_sem.at[5], across)
     send_back(3, 1, 2)
     exchange.wait()
+    block = (pl.ds(pl.multiple_of(core * rows + chip // 4 * 16, 16), 16), pl.ds(pl.multiple_of(chip % 4 * D, D), D))
     mine = home.at[CHIPS]
     mine[...] = (half[...] + pair[...]).astype(BF)
-    for_chips(lambda t, to: send(mine, gathered.at[0, chip], dw_sem.at[6], dw_sem.at[7], to))
+    for_chips(lambda t, to: send(mine, gathered.at[block], dw_sem.at[6], dw_sem.at[7], to))
     send_back(3, 2, 4)
-    wait(gathered.at[0], dw_sem.at[7])
-    send(gathered.at[0], gathered.at[1], dw_sem.at[8], dw_sem.at[9], other_core)
-
-    def write(owner, block):
-        for s in range(CHIPS):
-            where = pl.ds(pl.multiple_of(owner * rows + s // 4 * 16, 16), 16)
-            if s % 4 < 3:
-                dwqkv[where, s % 4 * D:s % 4 * D + D] = block[s].astype(F32)
-            else:
-                dwout[where, :] = block[s].astype(F32)
-
-    write(core, gathered.at[0])
-    wait(gathered.at[1], dw_sem.at[9])
-    write(1 - core, gathered.at[1])
+    wait(terms, dw_sem.at[7])
+    send(gathered.at[first], gathered.at[first], dw_sem.at[8], dw_sem.at[9], other_core)
 
     for c in range(PARTS):
         wait(staged.at[c], go_sem.at[c])
@@ -273,18 +262,19 @@
     wait(leaving, land_sem)
     wait(away.at[0], dw_sem.at[0])
     wait(terms, dw_sem.at[2])
-    wait(gathered.at[0], dw_sem.at[6])
-    wait(gathered.at[0], dw_sem.at[8])
+    wait(terms, dw_sem.at[6])
+    wait(terms, dw_sem.at[8])
+    wait(terms, dw_sem.at[9])
 
 
 def body(tokens, grad_out, w_qkv, w_out):
     shape = (MEM, PARTS, WIN, D)
     hbm, anywhere, vmem = (pl.BlockSpec(memory_space=space) for space in (pltpu.HBM, pl.ANY, pltpu.VMEM))
-    out, dwqkv, dwout = pl.pallas_call(
+    out, gathered = pl.pallas_call(
         kernel,
-        out_shape=(jax.ShapeDtypeStruct(shape, BF), jax.ShapeDtypeStruct((D, 3 * D), F32), jax.ShapeDtypeStruct((D, D), F32)),
+        out_shape=(jax.ShapeDtypeStruct(shape, BF), jax.ShapeDtypeStruct((D, 4 * D), BF)),
         in_specs=[hbm, hbm, hbm, hbm],
-        out_specs=(anywhere, vmem, vmem),
+        out_specs=(anywhere, vmem),
         scratch_shapes=[
             pltpu.VMEM((PARTS, MEM, WIN, 2 * D), BF),
             pltpu.VMEM((PARTS, MEM, WIN, 2 * D), BF),
@@ -306,7 +296,6 @@
             pltpu.VMEM((CHIPS, 16, D), BF),
             pltpu.VMEM((16, D), F32),
             pltpu.VMEM((16, D), F32),
-            pltpu.VMEM((2, CHIPS, 16, D), BF),
             pltpu.SemaphoreType.DMA((PARTS, 2)),
             pltpu.SemaphoreType.DMA((2,)),
             pltpu.SemaphoreType.DMA((PARTS,)),
@@ -318,7 +307,7 @@
         compiler_params=pltpu.CompilerParams(collective_id=0, has_side_effects=True, vmem_limit_bytes=48 << 20),
         name="grid_attention_backward",
     )(*(pltpu.with_memory_space_constraint(a, pltpu.HBM) for a in (tokens.reshape(shape), grad_out.reshape(shape), w_qkv, w_out)))
-    return out.reshape(tokens.shape), dwqkv, dwout
+    return out.reshape(tokens.shape), gathered[:, :3 * D].astype(F32), gathered[:, 3 * D:].astype(F32)
 
 
 def solution(mesh):

time: 93.5 us -> 93.1 us (level)
  other arithmetic: 0 us -> 1.65 us
  local copies, waits for them, and re-layouts: 2.9 us -> 1.32 us
    convert_element_type x0 -> x2, other arithmetic: none -> 1.65 us  [the longest x1 0.93 us: body(): gathered[:, :3 * D].astype(F32)]
    unnamed x3 -> x1, local copies, waits for them, and re-layouts: 2.9 us -> 1.32 us
where the time goes in v5:
time: 93.1 us; the launch traced here: 93 us
  Pallas kernels  89.4 us (96%)
  other arithmetic  1.65 us (2%)
  local copies, waits for them, and re-layouts  1.32 us (1%)
    pallas_call x1, Pallas kernels, body(): pl.pallas_call(kernel, out_shape=(jax.ShapeDtypeStruct(shape, BF), jax.Sh...  89.4 us

profile of v5, /device:TPU:1, one launch (start us, length us, event | category | flops | bytes accessed | tf_op | source)
XLA Modules:
  0.0 93.0 jit_solution(10524864454171988252)
XLA Ops:
  0.6 89.4 %grid_attention_backward.1 = (bf16[64,4,16,256]{3,2,1,0:T(8,128)(2,1)S(1)}, bf16[256,1024]{1,0:T(8,128)(2,1)S(1)}) custom-call(bf16[64,4,16,256]{3,2,1,0:T(8,128)(2,1)} %bitcast.4, bf16[64,4,16,256]{3,2,1,0:T(8,128)(2,1)} %bitcast.5, bf16[256,768]{1,0:T(8,128)(2,1)} %wqkv_hbm.1, bf16[256,256]{1,0:T(8,128)(2,1)} %wout_hbm.1), custom_call_target="tpu_custom_call" | custom-call | tf_op jit(solution)/shard_map/grid_attention_backward/pallas_call | solution.py:273
  90.0 0.7 slice_convert_fusion.1
  90.8 0.9 %slice_convert_fusion = f32[256,768]{1,0:T(8,128)} fusion(bf16[256,1024]{1,0:T(8,128)(2,1)S(1)} %get-tuple-element.6), kind=kLoop, calls=%fused_computation | loop fusion | flops 196608 | bytes 1179648 | tf_op jit(solution)/shard_map/convert_element_type | solution.py:310
  91.7 1.3 %copy.8 = bf16[16,16,16,256]{3,2,1,0:T(8,128)(2,1)} copy(bf16[16,16,16,256]{3,2,1,0:T(8,128)(2,1)S(1)} %bitcast.3) | data formatting | bytes 4194304

commit v6 on v4

--- a/solution.py
+++ b/solution.py
@@ -123,7 +123,7 @@
 
 def kernel(tok, grd, wqkv_hbm, wout_hbm, out, dwqkv, dwout, staged, arrived, leaving, wqkv, wout, swap, xw, gw, qkvg, grads,
            mix, dx, sbuf, pbuf, acc, away, home, terms, half, pair, gathered,
-           stage_sem, weight_sem, go_sem, come_sem, back_sem, land_sem, dw_sem):
+           stage_sem, weight_sem, go_sem, come_sem, back_sem, land_sem, dw_sem, gather_sem):
     y, gy, gz = lax.axis_index("gx"), lax.axis_index("gy"), lax.axis_index("gz")
     x_hi, core = gy // 2, gy % 2
     x, z_hi, z_lo = x_hi * 2 + gz // 4, gz % 4 // 2, gz % 2
@@ -157,7 +157,7 @@
             for d in range(4):
                 for z_of in (z_hi, 1 - z_hi):
                     y_of, (x_num, x_dev) = y_carry[d], x_part[d]
-                    act((y_of + x_num) // 2 + z_of, y_of * 2 + x_dev + device(0, 0, z_of, core, 0))
+                    act((y_of + x_num) // 2 + z_of, y_of * 2 + x_dev + device(0, 0, z_of, core, 0), i)
             return y_carry[1:] + y_carry[:1]
         lax.fori_loop(0, 4, outer, y_part)
 
@@ -219,7 +219,7 @@
             both = (acc[first, :] + away[1].astype(F32)).astype(BF)
             for s in range(CHIPS):
                 home[s] = both[s // 4 * 16:s // 4 * 16 + 16, s % 4 * D:s % 4 * D + D]
-            for_chips(lambda t, to: send(home.at[t], terms.at[chip], dw_sem.at[2], dw_sem.at[3], to))
+            for_chips(lambda t, to, i: send(home.at[t], terms.at[chip], dw_sem.at[2], dw_sem.at[3], to))
             send_back(2, 2, 4)
             send_back(3, 0, 1)
 
@@ -250,10 +250,13 @@
     exchange.wait()
     mine = home.at[CHIPS]
     mine[...] = (half[...] + pair[...]).astype(BF)
-    for_chips(lambda t, to: send(mine, gathered.at[0, chip], dw_sem.at[6], dw_sem.at[7], to))
+    for_chips(lambda t, to, i: send(mine, gathered.at[0, chip], dw_sem.at[6], gather_sem.at[i], to))
     send_back(3, 2, 4)
-    wait(gathered.at[0], dw_sem.at[7])
-    send(gathered.at[0], gathered.at[1], dw_sem.at[8], dw_sem.at[9], other_core)
+    for i in range(4):
+        wait(gathered.at[0, pl.ds(0, CHIPS // 4)], gather_sem.at[i])
+        for d in range(4):
+            chips = pl.ds((y_part[(-d - i) % 4] + x_part[-d % 4][0]) // 2, 2)
+            send(gathered.at[0, chips], gathered.at[1, chips], dw_sem.at[7], dw_sem.at[8], other_core)
 
     def write(owner, block):
         for s in range(CHIPS):
@@ -264,7 +267,7 @@
                 dwout[where, :] = block[s].astype(F32)
 
     write(core, gathered.at[0])
-    wait(gathered.at[1], dw_sem.at[9])
+    wait(gathered.at[1], dw_sem.at[8])
     write(1 - core, gathered.at[1])
 
     for c in range(PARTS):
@@ -274,7 +277,7 @@
     wait(away.at[0], dw_sem.at[0])
     wait(terms, dw_sem.at[2])
     wait(gathered.at[0], dw_sem.at[6])
-    wait(gathered.at[0], dw_sem.at[8])
+    wait(gathered.at[0], dw_sem.at[7])
 
 
 def body(tokens, grad_out, w_qkv, w_out):
@@ -313,7 +316,8 @@
             pltpu.SemaphoreType.DMA((PARTS,)),
             pltpu.SemaphoreType.DMA(()),
             pltpu.SemaphoreType.DMA(()),
-            pltpu.SemaphoreType.DMA((10,)),
+            pltpu.SemaphoreType.DMA((9,)),
+            pltpu.SemaphoreType.DMA((4,)),
         ],
         compiler_params=pltpu.CompilerParams(collective_id=0, has_side_effects=True, vmem_limit_bytes=48 << 20),
         name="grid_attention_backward",

time: 93.5 us -> 93.2 us (level)
  no operation moved by 1% of the time
where the time goes in v6:
time: 93.2 us; the launch traced here: 93.1 us
  Pallas kernels  89.5 us (96%)
  local copies, waits for them, and re-layouts  2.9 us (3%)
    pallas_call x1, Pallas kernels, body(): pl.pallas_call(kernel, out_shape=(jax.ShapeDtypeStruct(shape, BF), jax.Sh...  89.5 us
    unnamed x3, local copies, waits for them, and re-layouts  2.9 us

profile of v6, /device:TPU:1, one launch (start us, length us, event | category | flops | bytes accessed | tf_op | source)
XLA Modules:
  0.0 93.1 jit_solution(17634070950490082677)
XLA Ops:
  0.6 89.5 %grid_attention_backward.1 = (bf16[64,4,16,256]{3,2,1,0:T(8,128)(2,1)S(1)}, f32[256,768]{1,0:T(8,128)S(1)}, f32[256,256]{1,0:T(8,128)S(1)}) custom-call(bf16[64,4,16,256]{3,2,1,0:T(8,128)(2,1)} %bitcast.4, bf16[64,4,16,256]{3,2,1,0:T(8,128)(2,1)} %bitcast.5, bf16[256,768]{1,0:T(8,128)(2,1)} %wqkv_hbm.1, bf16[256,256]{1,0:T(8,128)(2,1)} %wout_hbm.1), custom_call_target="tpu_custom_call" | custom-call | tf_op jit(solution)/shard_map/grid_attention_backward/pallas_call | solution.py:286
  90.2 1.3 %copy.10 = bf16[16,16,16,256]{3,2,1,0:T(8,128)(2,1)} copy(bf16[16,16,16,256]{3,2,1,0:T(8,128)(2,1)S(1)} %bitcast.3) | data formatting | bytes 4194304
  91.5 0.9 copy.11
  92.4 0.7 copy.12
